TPU v7x, 32 devices: a whole 2x2x4 slice. The times are simulated.
32 devices in a mesh: groups: 2 (over y), seq: 4 (over z), query: 2 (over x), chan: 2 (over core).
Axes of the slice: x: 2, y: 2, z: 4, core: 2. Of those that a mesh axis runs over, the one named last changes fastest.
Arguments:
- hidden_rows: bfloat16 [4, 1024, 4096], P(('groups', 'query'), 'seq', 'chan'), parts along dimension 0, may hold values from -6 to 6
- scan_grad: bfloat16 [4, 1024, 8192], P(('groups', 'query'), 'seq', 'chan'), parts along dimension 0, may hold values from -6 to 6
- step_size: bfloat16 [4, 1024, 8192], P(('groups', 'query'), 'seq', 'chan'), parts along dimension 0, as said below
- state_proj: bfloat16 [4, 2, 16, 1024], P(('groups', 'query'), None, None, 'seq'), parts along dimension 0, may hold values from -6 to 6
- decay_rate: float32 [16, 8192], P(None, 'chan'), as said below
- skip_gain: float32 [8192], P('chan'), may hold values from 0.5 to 1.5
- in_sketch: bfloat16 [4096, 64], P('chan'), may hold values from -0.09375 to 0.09375
- out_sketch: bfloat16 [8192, 64], P('chan'), may hold values from -0.0625 to 0.0625
- doc_lengths: int32 [4, 8], P(('groups', 'query')), parts along dimension 0, may hold values from 1 to 512, 1024 in all within a row
- doc_slot: int32 [4, 8], P(('groups', 'query')), parts along dimension 0, may hold values from 0 to 7, each once within a row
- query_sketch: bfloat16 [32, 4096], P(('query', 'chan')), may hold values from -0.09375 to 0.09375
Outputs:
- scores: float32 [4, 8, 32], P(('groups', 'query'), 'seq'), parts along dimension 0
There are 2 independent parts, one for each index of `groups`. A program takes and returns all parts, laid end to end along the dimension named above; an argument that names none is the same for every part. Nothing has to cross between parts.
Inputs may be any that keep to these rules, and one draw needn't show every extreme that they name: `doc_lengths`: each row lists one sequence's documents in order; the lengths of a row sum to 1024 and the longest is exactly 512. `doc_slot`: each row names every slot once; slot k belongs to seq index k // 2. `step_size`: positive. `decay_rate`: positive.
All inputs are finite; a program needn't handle non-finite values.
Results may differ from a plain program's by a relative error of at most 0.0057.
Values may be sent and summed in bfloat16 or wider, within the bound.
A program may use at most 64 MiB of HBM per device.

v0:
```python
import jax
import jax.numpy as jnp
from jax import lax
from jax.sharding import PartitionSpec as P

SLOT = 2


tokens_per_turn = 8
rows_per_block = 8
epsilon = 1e-06


def shifted(block, axis, distance):
    devices = range(lax.axis_size(axis))
    route = [(i - distance, i) for i in devices if i - distance in devices]
    return lax.ppermute(block, axis, route)


def local_adjoint(
    grad_rows, step_rows, in_rows, out_rows, retain_mask, decay_rate, skip_gain, start_state
):
    row_total, channels = grad_rows.shape
    turn_count = row_total // tokens_per_turn
    blocks = (
        grad_rows.reshape(turn_count, tokens_per_turn, channels),
        step_rows.reshape(turn_count, tokens_per_turn, channels),
        in_rows.reshape(turn_count, tokens_per_turn, -1),
        out_rows.reshape(turn_count, tokens_per_turn, -1),
        retain_mask.reshape(turn_count, tokens_per_turn),
    )

    def one_turn(state_now, block_in):
        grad_block, step_block, in_block, out_block, keep_block = block_in
        results = [None] * tokens_per_turn
        for offset in reversed(range(tokens_per_turn)):
            grad_f = grad_block[offset].astype(jnp.float32)
            step_f = step_block[offset].astype(jnp.float32)
            adjoint = out_block[offset].astype(jnp.float32)[:, None] * grad_f[None, :] + state_now
            mixed = skip_gain * grad_f + step_f * jnp.sum(
                in_block[offset].astype(jnp.float32)[:, None] * adjoint, axis=0
            )
            results[offset] = mixed.astype(jnp.bfloat16)
            state_now = jnp.exp(-step_f[None, :] * decay_rate) * keep_block[offset] * adjoint
        return (state_now, jnp.stack(results))

    return lax.scan(one_turn, start_state, blocks, reverse=True)


def decayed_sum(grad_rows, step_rows, out_rows, retain_mask, decay_rate):
    row_total, channels = grad_rows.shape
    running_steps = jnp.cumsum(step_rows.astype(jnp.float32), axis=0)
    still_open = (jnp.cumsum(1.0 - retain_mask) == 0.0).astype(jnp.float32)
    weights = out_rows.astype(jnp.float32) * still_open[:, None]
    block_total = row_total // rows_per_block
    blocks = (
        grad_rows.reshape(block_total, rows_per_block, channels),
        running_steps.reshape(block_total, rows_per_block, channels),
        weights.reshape(block_total, rows_per_block, -1),
    )

    def add_block(total, block_in):
        grad_block, steps_block, weight_block = block_in
        factor = jnp.exp(-decay_rate[None, :, :] * steps_block[:, None, :])
        term = weight_block[:, :, None] * grad_block.astype(jnp.float32)[:, None, :] * factor
        return (total + jnp.sum(term, axis=0), None)

    total, _ = lax.scan(add_block, jnp.zeros(decay_rate.shape, jnp.float32), blocks)
    return (total, running_steps[-1])


def doc_sketch(entry_facet, out_side, positions, doc_starts, doc_ends, slot_pick):
    member_index = (
        (positions[:, None] >= doc_starts[None, :]) & (positions[:, None] < doc_ends[None, :])
    ).astype(jnp.float32)
    chosen = jnp.dot(member_index, slot_pick.T).astype(jnp.bfloat16)
    row_count = out_side.shape[0]
    weighted = (chosen[:, :, None] * out_side[:, None, :]).reshape(row_count, -1)
    product_sum = jnp.einsum("tk,tj->kj", weighted, entry_facet, preferred_element_type=jnp.float32)
    return product_sum.reshape(slot_pick.shape[0], -1)


def local(
    hidden_rows,
    scan_grad,
    step_size,
    state_proj,
    decay_rate,
    skip_gain,
    in_sketch,
    out_sketch,
    doc_lengths,
    doc_slot,
    query_sketch,
):
    tok_count = scan_grad.shape[1]
    seq_devices = lax.axis_size("seq")
    seq_index = lax.axis_index("seq")
    positions = seq_index * tok_count + jnp.arange(tok_count, dtype=jnp.int32)
    lengths_row = doc_lengths[0]
    doc_ends = jnp.cumsum(lengths_row)
    doc_starts = doc_ends - lengths_row
    retain_mask = 1.0 - jnp.any(positions[:, None] == doc_starts[None, :], axis=1).astype(
        jnp.float32
    )
    grad_rows = scan_grad[0]
    step_rows = step_size[0]
    in_rows = state_proj[0, 0].T
    out_rows = state_proj[0, 1].T
    zero_state = jnp.zeros(decay_rate.shape, jnp.float32)
    local_end, step_total = decayed_sum(grad_rows, step_rows, out_rows, retain_mask, decay_rate)
    through = jnp.exp(-decay_rate * step_total[None, :]) * jnp.prod(retain_mask)
    in_side_part = jnp.dot(hidden_rows[0], in_sketch, preferred_element_type=jnp.float32)

    def relay(turn_index, received):
        departing_rows = through * received + local_end
        return shifted(departing_rows, "seq", -1)

    incoming = lax.fori_loop(0, seq_devices - 1, relay, zero_state)
    _, input_grads = local_adjoint(
        grad_rows, step_rows, in_rows, out_rows, retain_mask, decay_rate, skip_gain, incoming
    )
    input_grads = input_grads.reshape(tok_count, -1)
    out_side_part = jnp.dot(input_grads, out_sketch, preferred_element_type=jnp.float32)
    entry_facet, out_side = lax.psum((in_side_part, out_side_part), "chan")
    entry_facet = entry_facet.astype(jnp.bfloat16)
    out_side = out_side.astype(jnp.bfloat16)
    slots_row = doc_slot[0]
    document_count = slots_row.shape[0]
    owned_slots = seq_index * SLOT + jnp.arange(SLOT, dtype=jnp.int32)
    own_pick = (slots_row[None, :] == owned_slots[:, None]).astype(jnp.float32)
    every_pick = jnp.eye(document_count, dtype=jnp.float32)
    doc_partial = doc_sketch(entry_facet, out_side, positions, doc_starts, doc_ends, every_pick)
    summed = lax.psum(doc_partial, "seq")
    own_sketch = jnp.dot(own_pick, summed, precision=lax.Precision.HIGHEST)
    mean_square = jnp.mean(own_sketch * own_sketch, axis=1, keepdims=True)
    normed = (own_sketch * lax.rsqrt(mean_square + epsilon)).astype(jnp.bfloat16)
    scores = lax.dot_general(
        normed,
        lax.all_gather(query_sketch, ("query", "chan"), axis=0, tiled=True),
        (((1,), (1,)), ((), ())),
        preferred_element_type=jnp.float32,
    )
    return scores[None]


def solution(mesh):
    placed = (
        P(("groups", "query"), "seq", "chan"),
        P(("groups", "query"), "seq", "chan"),
        P(("groups", "query"), "seq", "chan"),
        P(("groups", "query"), None, None, "seq"),
        P(None, "chan"),
        P("chan"),
        P("chan", None),
        P("chan", None),
        P(("groups", "query"), None),
        P(("groups", "query"), None),
        P(("query", "chan"), None),
    )
    return jax.shard_map(
        local,
        mesh=mesh,
        in_specs=placed,
        out_specs=P(("groups", "query"), "seq", None),
        check_vma=False,
    )
```

profile of v0, /device:TPU:0, one launch (start us, length us, event | category | flops | bytes accessed | tf_op | source)
XLA Modules:
  0.0 609.5 jit_solution(2833894429316115037)
XLA Ops:
  24.9 74.7 %while.41 = (s32[]{:T(128)}, f32[16,4096]{1,0:T(8,128)S(1)}, f32[32,8,16]{2,1,0:T(8,128)S(1)}, bf16[32,8,4096]{2,1,0:T(8,128)(2,1)}, f32[1,16,4096]{2,1,0:T(8,12...) while((s32[]{:T(128)}, f32[16,4096]{1,0:T(8,128)S(1)}, f32[32,8,16]{2,1,0:T(8,128)S(1)}, ...), condition=%wide.region_9.10_spmd.clone, body=%wide.region_7.9_spmd.clone.sunk | while | flops 2195459 | bytes 2033259 | solution.py:68
  100.0 29.2 %while.39 = (s32[]{:T(128)}, f32[16,4096]{1,0:T(8,128)S(1)}, f32[16,4096]{1,0:T(8,128)S(1)}, f32[16,4096]{1,0:T(8,128)S(1)}, s32[]{:T(128)}) while((s32[]{:T(128)}, f32[16,4096]{1,0:T(8,128)S(1)}, f32[16,4096]{1,0:T(8,128)S(1)}, f32[16,4096]{1,0:T(8,128)S(1)}, s32[]{:T(128)}) %tuple.150), condition=%wide.region_11.12_spmd, body=%wide.region_10.11_spmd.sunk | while | flops 131074 | bytes 2097253 | solution.py:119
  101.3 9.9 %collective-permute-done = f32[16,4096]{1,0:T(8,128)S(1)} collective-permute-done((f32[16,4096]{1,0:T(8,128)S(1)}, f32[16,4096]{1,0:T(8,128)S(1)}, u32[]{:S(2)}, u32[]{:S(2)}) %collective-permute-start) | collective-permute-done | bytes 262176 | tf_op jit(solution)/shard_map/while/body/eval_jaxpr/ppermute | solution.py:17
  112.6 8.1 %collective-permute-done = f32[16,4096]{1,0:T(8,128)S(1)} collective-permute-done((f32[16,4096]{1,0:T(8,128)S(1)}, f32[16,4096]{1,0:T(8,128)S(1)}, u32[]{:S(2)}, u32[]{:S(2)}) %collective-permute-start) | collective-permute-done | bytes 262176 | tf_op jit(solution)/shard_map/while/body/eval_jaxpr/ppermute | solution.py:17
  122.0 7.2 %collective-permute-done = f32[16,4096]{1,0:T(8,128)S(1)} collective-permute-done((f32[16,4096]{1,0:T(8,128)S(1)}, f32[16,4096]{1,0:T(8,128)S(1)}, u32[]{:S(2)}, u32[]{:S(2)}) %collective-permute-start) | collective-permute-done | bytes 262176 | tf_op jit(solution)/shard_map/while/body/eval_jaxpr/ppermute | solution.py:17
  130.8 427.2 %while.40 = (s32[]{:T(128)}, f32[16,4096]{1,0:T(8,128)S(1)}, bf16[32,8,4096]{2,1,0:T(8,128)(2,1)}, bf16[32,8,4096]{2,1,0:T(8,128)(2,1)}, f32[16,4096]{1,0:T(8,12...) while((s32[]{:T(128)}, f32[16,4096]{1,0:T(8,128)S(1)}, ...), condition=%wide.region_21.22_spmd, body=%wide.region_12.21_spmd.sunk | while | flops 4587786 | bytes 3821737 | solution.py:47
  136.5 3.4 multiply_reduce_fusion.14
  149.8 3.4 multiply_reduce_fusion.14
  163.0 3.4 multiply_reduce_fusion.14
  176.3 3.4 multiply_reduce_fusion.14
  189.5 3.4 multiply_reduce_fusion.14
  203.1 3.4 multiply_reduce_fusion.14
  216.4 3.4 multiply_reduce_fusion.14
  229.7 3.4 multiply_reduce_fusion.14
  243.2 3.4 multiply_reduce_fusion.14
  256.4 3.4 multiply_reduce_fusion.14
  269.7 3.4 multiply_reduce_fusion.14
  282.9 3.4 multiply_reduce_fusion.14
  296.3 3.4 multiply_reduce_fusion.14
  309.9 3.4 multiply_reduce_fusion.14
  323.4 3.4 multiply_reduce_fusion.14
  336.9 3.4 multiply_reduce_fusion.14
  350.1 3.4 multiply_reduce_fusion.14
  363.4 3.4 multiply_reduce_fusion.14
  376.9 3.4 multiply_reduce_fusion.14
  390.2 3.4 multiply_reduce_fusion.14
  403.7 3.4 multiply_reduce_fusion.14
  417.2 3.4 multiply_reduce_fusion.14
  457.2 3.4 multiply_reduce_fusion.14
  561.1 3.9 all-reduce.5
  566.0 5.9 all_gather.3
  571.9 28.6 %all-reduce.4.cloned.1.call-done = f32[8,4096]{1,0:T(8,128)} async-done(((f32[8,4096]{1,0:T(8,128)}), f32[8,4096]{1,0:T(8,128)}) %all-reduce.4.cloned.1.call-update) | async-done | bytes 131088 | tf_op jit(solution)/shard_map/psum | solution.py:134
  (618 shorter events, 448.9 us)
Async XLA Ops:
  6.5 553.9 %copy-start = (bf16[1,256,2048]{2,1,0:T(8,128)(2,1)S(1)}, bf16[1,256,2048]{2,1,0:T(8,128)(2,1)}, u32[]{:S(2)}) copy-start(bf16[1,256,2048]{2,1,0:T(8,128)(2,1)} %param.17) | copy-start | bytes 3145732
  6.5 594.0 %all-reduce.4.cloned.1.call-start = ((), (), s32[]{:S(2)}) async-start(), calls=%async_computation | async-start | bytes 262144 | tf_op jit(solution)/shard_map/psum | solution.py:134
  15.9 1.9 copy-start.2
  20.5 2.5 copy-start.1
  22.9 1.9 copy-start.3
  100.0 11.2 %collective-permute-start = (f32[16,4096]{1,0:T(8,128)S(1)}, f32[16,4096]{1,0:T(8,128)S(1)}, u32[]{:S(2)}, u32[]{:S(2)}) collective-permute-start(f32[16,4096]{1,0:T(8,128)S(1)} %multiply_add_fusion.12), channel_id=1, source_target_pairs={{4,0},{8,4},{12,8},{5,1},{9,5},{13,9},{6,2},{10,6},{14,10},{7,3},{... | collective-permute-start | bytes 786440 | tf_op jit(solution)/shard_map/while/body/eval_jaxpr/ppermute | solution.py:17
  111.3 9.4 %collective-permute-start = (f32[16,4096]{1,0:T(8,128)S(1)}, f32[16,4096]{1,0:T(8,128)S(1)}, u32[]{:S(2)}, u32[]{:S(2)}) collective-permute-start(f32[16,4096]{1,0:T(8,128)S(1)} %multiply_add_fusion.12), channel_id=1, source_target_pairs={{4,0},{8,4},{12,8},{5,1},{9,5},{13,9},{6,2},{10,6},{14,10},{7,3},{... | collective-permute-start | bytes 786440 | tf_op jit(solution)/shard_map/while/body/eval_jaxpr/ppermute | solution.py:17
  120.7 8.5 %collective-permute-start = (f32[16,4096]{1,0:T(8,128)S(1)}, f32[16,4096]{1,0:T(8,128)S(1)}, u32[]{:S(2)}, u32[]{:S(2)}) collective-permute-start(f32[16,4096]{1,0:T(8,128)S(1)} %multiply_add_fusion.12), channel_id=1, source_target_pairs={{4,0},{8,4},{12,8},{5,1},{9,5},{13,9},{6,2},{10,6},{14,10},{7,3},{... | collective-permute-start | bytes 786440 | tf_op jit(solution)/shard_map/while/body/eval_jaxpr/ppermute | solution.py:17
  129.2 1.6 copy-start.5
  130.8 427.2 %copy-start.4 = (bf16[4096,64]{0,1:T(8,128)(2,1)S(1)}, bf16[4096,64]{0,1:T(8,128)(2,1)}, u32[]{:S(2)}) copy-start(bf16[4096,64]{0,1:T(8,128)(2,1)} %param.24) | copy-start | bytes 1572868
  558.0 2.4 copy-start.6
  560.4 5.6 copy-start.7
  560.5 40.0 %copy-start.8 = (s32[1,8]{1,0:T(1,128)S(1)}, s32[1,8]{1,0:T(1,128)}, u32[]{:S(2)}) copy-start(s32[1,8]{1,0:T(1,128)} %param.26) | copy-start | bytes 100
Sparse Core Ops, SparseCore 0:
  566.1 34.3 all-reduce.3
where the time goes:
time: 622 us; the launch traced here: 609 us
  other arithmetic  431 us (69%)
  local copies, waits for them, and re-layouts  87.8 us (14%)
  waiting for transfers between devices  53.8 us (9%)
  between operations  13.6 us (2%)
  blocking collectives  9.71 us (2%)
    reduce_sum x64, other arithmetic, one_turn(): jnp.sum(in_block[offset].astype(jnp.float32)[:, None] * adjoint, axis=0)  182 us
    convert_element_type x32, other arithmetic, one_turn(): results[offset] = mixed.astype(jnp.bfloat16)  62.7 us
    neg x32, other arithmetic, one_turn(): -step_f[None, :] * decay_rate  44.5 us
    convert_element_type x32, other arithmetic, one_turn(): grad_f = grad_block[offset].astype(jnp.float32)  43.4 us
    mul x32, other arithmetic, one_turn(): jnp.exp(-step_f[None, :] * decay_rate) * keep_block[offset] * adjoint  42.8 us
    mul x32, local copies, waits for them, and re-layouts, add_block(): factor = jnp.exp(-decay_rate[None, :, :] * steps_block[:, None, :])  29.4 us
    psum x1, waiting for transfers between devices, local(): summed = lax.psum(doc_partial, 'seq')  28.6 us
    convert_element_type x32, other arithmetic, add_block(): grad_block.astype(jnp.float32)[:, None, :]  27.3 us
  transfers between devices with their start and end apart: 4, of which 4 were waited for; matrix products, arithmetic and copies ran while one was open for 0% of the time, Pallas kernels for 0%

commit v1 on v0

v1 whole, which is shorter than its diff:
```python
import math

import jax
import jax.numpy as jnp
from jax import lax
from jax.experimental import pallas as pl
from jax.experimental.pallas import tpu as pltpu
from jax.sharding import PartitionSpec as P

SLOT = 2
epsilon = 1e-06
LANES = 128
GROUP = 16
CHUNK = 1024
TINY = 1.1754944e-38


def lane_tiles(width):
    return [slice(t * LANES, (t + 1) * LANES) for t in range(width // LANES)]


def scan_kernel(grad, step, rate, out_table, in_diag, reset, y, carry_out, step_f, grad_f, states):
    rows, width = grad.shape
    count = rate.shape[0]
    tiles = lane_tiles(width)
    step_f[...] = step[...].astype(jnp.float32) + reset[...]
    grad_f[...] = grad[...].astype(jnp.float32)
    rates = [rate[:, t] for t in tiles]

    def one_group(index, carry):
        group = rows // GROUP - 1 - index
        first = pl.multiple_of(group * GROUP, GROUP)
        near_step = step_f.at[pl.ds(first, GROUP), :]
        near_grad = grad_f.at[pl.ds(first, GROUP), :]
        for offset in reversed(range(GROUP)):
            row = first + offset
            weight = out_table[pl.ds(pl.multiple_of(row * count, count), count), :]
            fresh = []
            for t, a, held in zip(tiles, rates, carry):
                adjoint = weight * near_grad[offset : offset + 1, t] + held
                states[offset * count : (offset + 1) * count, t] = adjoint.astype(jnp.bfloat16)
                fresh.append(jnp.exp2(near_step[offset : offset + 1, t] * a) * adjoint)
            carry = fresh
        y[pl.ds(first, GROUP), :] = jnp.dot(
            in_diag[pl.ds(first, GROUP), :], states[...], preferred_element_type=jnp.float32
        )
        return carry

    start = [jnp.zeros((count, LANES), jnp.float32) for _ in tiles]
    last = lax.fori_loop(0, rows // GROUP, one_group, start)
    for t, value in zip(tiles, last):
        carry_out[:, t] = value


def join_kernel(
    grad, step, rate, in_diag, later, skip, y, incoming, sketch, side, suffix, states, mixed
):
    rows, width = grad.shape
    count = rate.shape[0]
    tiles = lane_tiles(width)
    suffix[...] = jnp.dot(later[...], step[...], preferred_element_type=jnp.float32)
    rates = [rate[:, t] for t in tiles]
    enters = [incoming[:, t] for t in tiles]

    def one_group(group, _):
        first = pl.multiple_of(group * GROUP, GROUP)
        near = suffix.at[pl.ds(first, GROUP), :]
        for offset in range(GROUP):
            one = slice(offset, offset + 1)
            for t, a, e in zip(tiles, rates, enters):
                value = jnp.exp2(near[one, t] * a) * e
                states[offset * count : (offset + 1) * count, t] = value.astype(jnp.bfloat16)
        added = jnp.dot(
            in_diag[pl.ds(first, GROUP), :], states[...], preferred_element_type=jnp.float32
        )
        here = pl.ds(first, GROUP)
        total = y[here, :] + added
        result = skip[...] * grad[here, :].astype(jnp.float32) + step[here, :].astype(
            jnp.float32
        ) * total
        mixed[here, :] = result.astype(jnp.bfloat16)
        return 0

    lax.fori_loop(0, rows // GROUP, one_group, 0)
    part = jnp.dot(mixed[...], sketch[...], preferred_element_type=jnp.float32)

    @pl.when(pl.program_id(0) == 0)
    def _():
        side[...] = part

    @pl.when(pl.program_id(0) > 0)
    def _():
        side[...] += part


def whole(shape):
    return pl.BlockSpec(shape, lambda i: (0,) * len(shape))


def columns(height, width):
    return pl.BlockSpec((height, width), lambda i: (0, i))


def run_scan(grad, step, rate, out_table, in_diag, reset):
    rows, channels = grad.shape
    count = rate.shape[0]
    return pl.pallas_call(
        scan_kernel,
        grid=(channels // CHUNK,),
        in_specs=[
            columns(rows, CHUNK),
            columns(rows, CHUNK),
            columns(count, CHUNK),
            whole(out_table.shape),
            whole(in_diag.shape),
            whole(reset.shape),
        ],
        out_specs=[columns(rows, CHUNK), columns(count, CHUNK)],
        out_shape=[
            jax.ShapeDtypeStruct((rows, channels), jnp.float32),
            jax.ShapeDtypeStruct((count, channels), jnp.float32),
        ],
        scratch_shapes=[
            pltpu.VMEM((rows, CHUNK), jnp.float32),
            pltpu.VMEM((rows, CHUNK), jnp.float32),
            pltpu.VMEM((GROUP * count, CHUNK), jnp.bfloat16),
        ],
        compiler_params=pltpu.CompilerParams(vmem_limit_bytes=48 * 2**20),
        name="scan",
    )(grad, step, rate, out_table, in_diag, reset)


def run_join(grad, step, rate, in_diag, later, skip, y, incoming, sketch):
    rows, channels = grad.shape
    count = rate.shape[0]
    return pl.pallas_call(
        join_kernel,
        grid=(channels // CHUNK,),
        in_specs=[
            columns(rows, CHUNK),
            columns(rows, CHUNK),
            columns(count, CHUNK),
            whole(in_diag.shape),
            whole(later.shape),
            columns(1, CHUNK),
            columns(rows, CHUNK),
            columns(count, CHUNK),
            pl.BlockSpec((CHUNK, sketch.shape[1]), lambda i: (i, 0)),
        ],
        out_specs=whole((rows, sketch.shape[1])),
        out_shape=jax.ShapeDtypeStruct((rows, sketch.shape[1]), jnp.float32),
        scratch_shapes=[
            pltpu.VMEM((rows, CHUNK), jnp.float32),
            pltpu.VMEM((GROUP * count, CHUNK), jnp.bfloat16),
            pltpu.VMEM((rows, CHUNK), jnp.bfloat16),
        ],
        compiler_params=pltpu.CompilerParams(vmem_limit_bytes=48 * 2**20),
        name="join",
    )(grad, step, rate, in_diag, later, skip, y, incoming, sketch)


def shifted(block, axis, distance):
    devices = range(lax.axis_size(axis))
    route = [(i - distance, i) for i in devices if i - distance in devices]
    return lax.ppermute(block, axis, route)


def doc_sketch(entry_facet, out_side, positions, doc_starts, doc_ends, slot_pick):
    member_index = (
        (positions[:, None] >= doc_starts[None, :]) & (positions[:, None] < doc_ends[None, :])
    ).astype(jnp.float32)
    chosen = jnp.dot(member_index, slot_pick.T).astype(jnp.bfloat16)
    row_count = out_side.shape[0]
    weighted = (chosen[:, :, None] * out_side[:, None, :]).reshape(row_count, -1)
    product_sum = jnp.einsum("tk,tj->kj", weighted, entry_facet, preferred_element_type=jnp.float32)
    return product_sum.reshape(slot_pick.shape[0], -1)


def local(
    hidden_rows,
    scan_grad,
    step_size,
    state_proj,
    decay_rate,
    skip_gain,
    in_sketch,
    out_sketch,
    doc_lengths,
    doc_slot,
    query_sketch,
):
    tok_count = scan_grad.shape[1]
    seq_devices = lax.axis_size("seq")
    seq_index = lax.axis_index("seq")
    positions = seq_index * tok_count + jnp.arange(tok_count, dtype=jnp.int32)
    lengths_row = doc_lengths[0]
    doc_ends = jnp.cumsum(lengths_row)
    doc_starts = doc_ends - lengths_row
    retain_mask = 1.0 - jnp.any(positions[:, None] == doc_starts[None, :], axis=1).astype(
        jnp.float32
    )
    grad_rows = scan_grad[0]
    step_rows = step_size[0]
    count = decay_rate.shape[0]
    rate = -jnp.maximum(decay_rate * math.log2(math.e), TINY)
    reset = jnp.where(retain_mask > 0.0, 0.0, jnp.inf).astype(jnp.float32)[:, None]
    out_table = jnp.broadcast_to(
        state_proj[0, 1].T.astype(jnp.float32)[:, :, None], (tok_count, count, LANES)
    ).reshape(tok_count * count, LANES)
    line = jnp.arange(tok_count, dtype=jnp.int32)
    place = jnp.arange(GROUP * count, dtype=jnp.int32)
    on_line = (line[:, None] % GROUP) == (place[None, :] // count)
    in_wide = jnp.tile(state_proj[0, 0].T, (1, GROUP))
    in_diag = jnp.where(on_line, in_wide, 0).astype(jnp.bfloat16)
    still_open = jnp.flip(jnp.cumprod(jnp.flip(jnp.roll(retain_mask, -1).at[-1].set(1.0))))
    in_open = jnp.where(still_open[:, None] > 0.0, in_diag, 0).astype(jnp.bfloat16)
    later = (line[:, None] < line[None, :]).astype(jnp.bfloat16)
    y, local_end = run_scan(grad_rows, step_rows, rate, out_table, in_diag, reset)
    step_total = jnp.sum(step_rows.astype(jnp.float32), axis=0)
    through = jnp.exp2(rate * step_total[None, :]) * jnp.prod(retain_mask)
    in_side_part = jnp.dot(hidden_rows[0], in_sketch, preferred_element_type=jnp.float32)

    def relay(turn_index, received):
        departing_rows = through * received + local_end
        return shifted(departing_rows, "seq", -1)

    incoming = lax.fori_loop(0, seq_devices - 1, relay, jnp.zeros_like(local_end))
    out_side_part = run_join(
        grad_rows, step_rows, rate, in_open, later, skip_gain[None, :], y, incoming, out_sketch
    )
    entry_facet, out_side = lax.psum((in_side_part, out_side_part), "chan")
    entry_facet = entry_facet.astype(jnp.bfloat16)
    out_side = out_side.astype(jnp.bfloat16)
    slots_row = doc_slot[0]
    document_count = slots_row.shape[0]
    owned_slots = seq_index * SLOT + jnp.arange(SLOT, dtype=jnp.int32)
    own_pick = (slots_row[None, :] == owned_slots[:, None]).astype(jnp.float32)
    every_pick = jnp.eye(document_count, dtype=jnp.float32)
    doc_partial = doc_sketch(entry_facet, out_side, positions, doc_starts, doc_ends, every_pick)
    summed = lax.psum(doc_partial, "seq")
    own_sketch = jnp.dot(own_pick, summed, precision=lax.Precision.HIGHEST)
    mean_square = jnp.mean(own_sketch * own_sketch, axis=1, keepdims=True)
    normed = (own_sketch * lax.rsqrt(mean_square + epsilon)).astype(jnp.bfloat16)
    scores = lax.dot_general(
        normed,
        lax.all_gather(query_sketch, ("query", "chan"), axis=0, tiled=True),
        (((1,), (1,)), ((), ())),
        preferred_element_type=jnp.float32,
    )
    return scores[None]


def solution(mesh):
    placed = (
        P(("groups", "query"), "seq", "chan"),
        P(("groups", "query"), "seq", "chan"),
        P(("groups", "query"), "seq", "chan"),
        P(("groups", "query"), None, None, "seq"),
        P(None, "chan"),
        P("chan"),
        P("chan", None),
        P("chan", None),
        P(("groups", "query"), None),
        P(("groups", "query"), None),
        P(("query", "chan"), None),
    )
    return jax.shard_map(
        local,
        mesh=mesh,
        in_specs=placed,
        out_specs=P(("groups", "query"), "seq", None),
        check_vma=False,
    )
```

time: 622 us -> 175 us (0.28); the launches traced: 609 us -> 174 us
  other arithmetic: 431 us -> 17.6 us
  local copies, waits for them, and re-layouts: 87.8 us -> 13.8 us
  Pallas kernels: 0 us -> 56.4 us
    reduce_sum x96 -> x1, other arithmetic: 196 us -> 2.53 us  [local(): step_total = jnp.sum(step_rows.astype(jnp.float32), axis=0)]
    convert_element_type x161 -> x1, other arithmetic: 134 us -> 0.02 us  [local(): later = (line[:, None] < line[None, :]).astype(jnp.bfloat16)]
    pallas_call x0 -> x2, Pallas kernels: none -> 56.4 us  [the longest x1 29.6 us: run_scan(): pl.pallas_call(scan_kernel, grid=(channels // CHUNK,), in_specs=[columns(...]
    neg x33 -> x0, other arithmetic: 45.3 us -> none  [the longest x32 44.5 us: one_turn(): -step_f[None, :] * decay_rate]
    mul x33 -> x2, other arithmetic: 43.5 us -> 2.59 us  [the longest x1 2.51 us: local(): through = jnp.exp2(rate * step_total[None, :]) * jnp.prod(retain_mask)]
    mul x65 -> x0, local copies, waits for them, and re-layouts: 29.8 us -> none  [the longest x32 29.4 us: add_block(): factor = jnp.exp(-decay_rate[None, :, :] * steps_block[:, None, :])]
    slice x33 -> x2, local copies, waits for them, and re-layouts: 21.6 us -> 0.61 us  [local(): jnp.roll(retain_mask, -1).at[-1].set(1.0)]
    dynamic_update_slice x32 -> x0, local copies, waits for them, and re-layouts: 20.1 us -> none  [local_adjoint(): return lax.scan(one_turn, start_state, blocks, reverse=True)]
where the time goes in v1:
time: 175 us; the launch traced here: 174 us
  Pallas kernels  56.4 us (32%)
  waiting for transfers between devices  54.8 us (31%)
  other arithmetic  17.6 us (10%)
  local copies, waits for them, and re-layouts  13.8 us (8%)
  between operations  13.5 us (8%)
  blocking collectives  10.6 us (6%)
  starting transfers between devices  3.84 us (2%)
  matrix products  3.62 us (2%)
    pallas_call x1, Pallas kernels, run_scan(): pl.pallas_call(scan_kernel, grid=(channels // CHUNK,), in_specs=[columns(...  29.6 us
    psum x1, waiting for transfers between devices, local(): summed = lax.psum(doc_partial, 'seq')  28.6 us
    pallas_call x1, Pallas kernels, run_join(): pl.pallas_call(join_kernel, grid=(channels // CHUNK,), in_specs=[columns(...  26.8 us
    ppermute x3, waiting for transfers between devices, shifted(): return lax.ppermute(block, axis, route)  26.1 us
    unnamed x31, local copies, waits for them, and re-layouts  7.51 us
    all_gather x1, blocking collectives, local(): lax.all_gather(query_sketch, ('query', 'chan'), axis=0, tiled=True)  5.87 us
    add x3, other arithmetic, relay(): departing_rows = through * received + local_end  5.5 us
    psum x1, blocking collectives, local(): entry_facet, out_side = lax.psum((in_side_part, out_side_part), 'chan')  4.71 us
  transfers between devices with their start and end apart: 4, of which 4 were waited for; matrix products, arithmetic and copies ran while one was open for 0% of the time, Pallas kernels for 0%

profile of v1, /device:TPU:0, one launch (start us, length us, event | category | flops | bytes accessed | tf_op | source)
XLA Modules:
  0.0 174.1 jit_solution(7954736908795078668)
XLA Ops:
  6.5 0.9 reduce-window.11
  12.7 0.7 convert_bitcast_fusion
  13.5 0.7 copy.27
  14.2 2.5 %convert_reduce_fusion = f32[4096]{0:T(1024)} fusion(bf16[1,256,4096]{2,1,0:T(8,128)(2,1)} %param.17), kind=kLoop, calls=%fused_computation.1 | loop fusion | flops 2093056 | bytes 2113536 | tf_op jit(solution)/shard_map/reduce_sum | solution.py:219
  16.7 0.8 copy.29.reset
  17.7 2.5 %copy.30.sketch = bf16[4096,64]{1,0:T(8,128)(2,1)} copy(bf16[4096,64]{0,1:T(8,128)(2,1)} %param.22) | data formatting | bytes 1048576 | tf_op args[7]
  20.3 2.5 %exponential_multiply_fusion = (f32[16,4096]{1,0:T(8,128)}, f32[16,4096]{1,0:T(8,128)S(1)}) fusion(f32[]{:T(128)} %get-tuple-element.60, f32[4096]{0:T(1024)} %convert_reduce_fusion, f32[16,4096]{1,0:T(8,128)} %param.19), kind=kLoop, calls=%fused_computation.6 | loop fusion | flops 393216 | bytes 802820 | tf_op jit(solution)/shard_map/mul | solution.py:220
  22.8 1.7 broadcast_select_fusion
  24.5 1.9 %broadcast_in_dim.37.out_table = f32[4096,128]{1,0:T(8,128)} broadcast(f32[4096]{0:T(1024)S(1)} %reshape.167), dimensions={0} | broadcast | bytes 2113536 | tf_op jit(solution)/shard_map/broadcast_in_dim | solution.py:207
  26.4 29.6 %scan.1 = (f32[256,4096]{1,0:T(8,128)}, f32[16,4096]{1,0:T(8,128)}) custom-call(bf16[256,4096]{1,0:T(8,128)(2,1)S(1)} %bitcast.40, bf16[256,4096]{1,0:T(8,128)(2,1)S(1)} %bitcast.38, f32[16,4096]{1,0:T(8,128)S(1)} %get-tuple-element.57.rate, f32[4096,128]{1,0:T(8,128)} %broadcast_in_dim.37.out_table, bf16[256,256]{1,0:T(8,128)(2,1)S(1)} %get-tuple-element.55.in_diag, ...), custom_call_target="tpu_custom_call" | custom-call | tf_op jit(solution)/shard_map/scan/pallas_call | solution.py:107
  56.0 0.7 broadcast_in_dim.63
  56.8 35.5 %while.11 = (s32[]{:T(128)}, f32[16,4096]{1,0:T(8,128)}, f32[16,4096]{1,0:T(8,128)}, f32[16,4096]{1,0:T(8,128)}, s32[]{:T(128)}) while((s32[]{:T(128)}, f32[16,4096]{1,0:T(8,128)}, f32[16,4096]{1,0:T(8,128)}, f32[16,4096]{1,0:T(8,128)}, s32[]{:T(128)}) %tuple.29), condition=%wide.region_7.8_spmd, body=%wide.region_6.7_spmd.sunk | while | flops 131074 | bytes 2097253 | solution.py:227
  56.8 1.8 %multiply_add_fusion.2 = f32[16,4096]{1,0:T(8,128)} fusion(f32[16,4096]{1,0:T(8,128)} %get-tuple-element.105, f32[16,4096]{1,0:T(8,128)} %get-tuple-element.104, f32[16,4096]{1,0:T(8,128)} %get-tuple-element.98), kind=kLoop, calls=%fused_computation.clone.1 | loop fusion | flops 131072 | bytes 1048576 | tf_op jit(solution)/shard_map/while/body/eval_jaxpr/add | solution.py:224
  58.6 1.3 collective-permute-start
  59.9 10.2 %collective-permute-done = f32[16,4096]{1,0:T(8,128)} collective-permute-done((f32[16,4096]{1,0:T(8,128)}, f32[16,4096]{1,0:T(8,128)}, u32[]{:S(2)}, u32[]{:S(2)}) %collective-permute-start) | collective-permute-done | bytes 262176 | tf_op jit(solution)/shard_map/while/body/eval_jaxpr/ppermute | solution.py:165
  70.1 1.8 %multiply_add_fusion.2 = f32[16,4096]{1,0:T(8,128)} fusion(f32[16,4096]{1,0:T(8,128)} %get-tuple-element.105, f32[16,4096]{1,0:T(8,128)} %get-tuple-element.104, f32[16,4096]{1,0:T(8,128)} %get-tuple-element.98), kind=kLoop, calls=%fused_computation.clone.1 | loop fusion | flops 131072 | bytes 1048576 | tf_op jit(solution)/shard_map/while/body/eval_jaxpr/add | solution.py:224
  72.0 1.3 collective-permute-start
  73.3 8.4 %collective-permute-done = f32[16,4096]{1,0:T(8,128)} collective-permute-done((f32[16,4096]{1,0:T(8,128)}, f32[16,4096]{1,0:T(8,128)}, u32[]{:S(2)}, u32[]{:S(2)}) %collective-permute-start) | collective-permute-done | bytes 262176 | tf_op jit(solution)/shard_map/while/body/eval_jaxpr/ppermute | solution.py:165
  81.7 1.8 %multiply_add_fusion.2 = f32[16,4096]{1,0:T(8,128)} fusion(f32[16,4096]{1,0:T(8,128)} %get-tuple-element.105, f32[16,4096]{1,0:T(8,128)} %get-tuple-element.104, f32[16,4096]{1,0:T(8,128)} %get-tuple-element.98), kind=kLoop, calls=%fused_computation.clone.1 | loop fusion | flops 131072 | bytes 1048576 | tf_op jit(solution)/shard_map/while/body/eval_jaxpr/add | solution.py:224
  83.5 1.3 collective-permute-start
  84.8 7.5 %collective-permute-done = f32[16,4096]{1,0:T(8,128)} collective-permute-done((f32[16,4096]{1,0:T(8,128)}, f32[16,4096]{1,0:T(8,128)}, u32[]{:S(2)}, u32[]{:S(2)}) %collective-permute-start) | collective-permute-done | bytes 262176 | tf_op jit(solution)/shard_map/while/body/eval_jaxpr/ppermute | solution.py:165
  92.3 1.6 copy-done.3
  93.9 1.2 copy-done.4
  95.1 0.9 copy-done.5
  96.0 26.8 %join.1 = f32[256,64]{1,0:T(8,128)S(1)} custom-call(bf16[256,4096]{1,0:T(8,128)(2,1)S(1)} %bitcast.41, bf16[256,4096]{1,0:T(8,128)(2,1)S(1)} %bitcast.39, f32[16,4096]{1,0:T(8,128)S(1)} %get-tuple-element.57.rate, bf16[256,256]{1,0:T(8,128)(2,1)S(1)} %copy-done.5, bf16[256,256]{1,0:T(8,128)(2,1)S(1)} %fusion.2.later, f32[1,4096]{1,0:T(1,128)S(1)} %bitcast.42, ...), custom_call_target="tpu_custom_call" | custom-call | tf_op jit(solution)/shard_map/join/pallas_call | solution.py:136
  123.9 4.7 %all-reduce.5 = (bf16[256,64]{1,0:T(8,128)(2,1)S(1)}, bf16[256,64]{0,1:T(8,128)(2,1)S(1)}) all-reduce(f32[256,64]{1,0:T(8,128)} %copy-done.6, f32[256,64]{0,1:T(8,128)S(1)} %fusion), channel_id=1, replica_groups=mesh['groups'=2,'seq'=4,'query'=2,'chan'=2] {'chan'}, use_global_device_ids=true, to_apply=%region_8.9 | all-reduce | flops 32768 | bytes 196608 | tf_op jit(solution)/shard_map/psum | solution.py:231
  128.7 0.9 convolution_convert_fusion
  129.8 0.8 reshape.166
  130.6 5.9 %all_gather.3 = bf16[32,4096]{1,0:T(8,128)(2,1)S(1)} all-gather(bf16[8,4096]{1,0:T(8,128)(2,1)S(1)} %copy-done.10), channel_id=1, replica_groups=mesh['groups'=2,'seq'=4,'query'=2,'chan'=2] {'query','chan'}, dimensions={0}, use_global_device_ids=true | all-gather | bytes 327680 | tf_op jit(solution)/shard_map/all_gather | solution.py:246
  136.5 28.6 %all-reduce.4.cloned.1.call-done = f32[8,4096]{1,0:T(8,128)} async-done(((f32[8,4096]{1,0:T(8,128)}), f32[8,4096]{1,0:T(8,128)}) %all-reduce.4.cloned.1.call-update) | async-done | bytes 131088 | tf_op jit(solution)/shard_map/psum | solution.py:240
  165.1 1.3 multiply_reduce_fusion
  166.4 0.8 convolution_bitcast_fusion
  (56 shorter events, 6.9 us)
Async XLA Ops:
  6.5 116.9 %copy-start = (bf16[1,256,2048]{2,1,0:T(8,128)(2,1)S(1)}, bf16[1,256,2048]{2,1,0:T(8,128)(2,1)}, u32[]{:S(2)}) copy-start(bf16[1,256,2048]{2,1,0:T(8,128)(2,1)} %param.15) | copy-start | bytes 3145732
  6.5 158.6 %all-reduce.4.cloned.1.call-start = ((), (), s32[]{:S(2)}) async-start(), calls=%async_computation | async-start | bytes 262144 | tf_op jit(solution)/shard_map/psum | solution.py:240
  7.5 2.6 %copy-start.14 = (s32[8,1]{0,1:T(1,128)}, s32[8,1]{0,1:T(1,128)S(1)}, u32[]{:S(2)}) copy-start(s32[8,1]{0,1:T(1,128)S(1)} %reduce-window.11) | copy-start | bytes 100
  8.1 1.9 %copy-start.13 = (s32[8]{0:T(128)}, s32[8]{0:T(128)S(1)}, u32[]{:S(2)}) copy-start(s32[8]{0:T(128)S(1)} %fusion.14) | copy-start | bytes 100
  8.1 0.6 copy-start.11
  17.7 8.7 %copy-start.1 = (bf16[1,256,4096]{2,1,0:T(8,128)(2,1)S(1)}, bf16[1,256,4096]{2,1,0:T(8,128)(2,1)}, u32[]{:S(2)}) copy-start(bf16[1,256,4096]{2,1,0:T(8,128)(2,1)} %param.17) | copy-start | bytes 6291460
  20.3 6.1 %copy-start.2 = (bf16[1,256,4096]{2,1,0:T(8,128)(2,1)S(1)}, bf16[1,256,4096]{2,1,0:T(8,128)(2,1)}, u32[]{:S(2)}) copy-start(bf16[1,256,4096]{2,1,0:T(8,128)(2,1)} %param.16) | copy-start | bytes 6291460
  20.3 6.1 %copy-start.7 = (f32[256,1]{1,0:T(8,128)S(1)}, f32[256,1]{1,0:T(8,128)}, u32[]{:S(2)}) copy-start(f32[256,1]{1,0:T(8,128)} %copy.29.reset) | copy-start | bytes 3076
  56.8 35.5 %copy-start.8 = (f32[4096]{0:T(1024)S(1)}, f32[4096]{0:T(1024)}, u32[]{:S(2)}) copy-start(f32[4096]{0:T(1024)} %param.20) | copy-start | bytes 49156
  58.6 11.5 %collective-permute-start = (f32[16,4096]{1,0:T(8,128)}, f32[16,4096]{1,0:T(8,128)}, u32[]{:S(2)}, u32[]{:S(2)}) collective-permute-start(f32[16,4096]{1,0:T(8,128)} %multiply_add_fusion.2), channel_id=1, source_target_pairs={{4,0},{8,4},{12,8},{5,1},{9,5},{13,9},{6,2},{10,6},{14,10},{7,3},{... | collective-permute-start | bytes 786440 | tf_op jit(solution)/shard_map/while/body/eval_jaxpr/ppermute | solution.py:165
  72.0 9.7 %collective-permute-start = (f32[16,4096]{1,0:T(8,128)}, f32[16,4096]{1,0:T(8,128)}, u32[]{:S(2)}, u32[]{:S(2)}) collective-permute-start(f32[16,4096]{1,0:T(8,128)} %multiply_add_fusion.2), channel_id=1, source_target_pairs={{4,0},{8,4},{12,8},{5,1},{9,5},{13,9},{6,2},{10,6},{14,10},{7,3},{... | collective-permute-start | bytes 786440 | tf_op jit(solution)/shard_map/while/body/eval_jaxpr/ppermute | solution.py:165
  83.5 8.8 %collective-permute-start = (f32[16,4096]{1,0:T(8,128)}, f32[16,4096]{1,0:T(8,128)}, u32[]{:S(2)}, u32[]{:S(2)}) collective-permute-start(f32[16,4096]{1,0:T(8,128)} %multiply_add_fusion.2), channel_id=1, source_target_pairs={{4,0},{8,4},{12,8},{5,1},{9,5},{13,9},{6,2},{10,6},{14,10},{7,3},{... | collective-permute-start | bytes 786440 | tf_op jit(solution)/shard_map/while/body/eval_jaxpr/ppermute | solution.py:165
  92.3 1.6 copy-start.3
  93.9 1.2 copy-start.4
  95.1 0.9 copy-start.5
  96.0 27.5 %copy-start.9 = (bf16[2048,64]{0,1:T(8,128)(2,1)S(1)}, bf16[2048,64]{0,1:T(8,128)(2,1)}, u32[]{:S(2)}) copy-start(bf16[2048,64]{0,1:T(8,128)(2,1)} %param.21) | copy-start | bytes 786436
  122.8 0.6 copy-start.6
  123.4 7.2 %copy-start.10 = (bf16[8,4096]{1,0:T(8,128)(2,1)S(1)}, bf16[8,4096]{1,0:T(8,128)(2,1)}, u32[]{:S(2)}) copy-start(bf16[8,4096]{1,0:T(8,128)(2,1)} %param.25) | copy-start | bytes 196612
  123.4 41.7 %copy-start.12 = (s32[1,8]{1,0:T(1,128)S(1)}, s32[1,8]{1,0:T(1,128)}, u32[]{:S(2)}) copy-start(s32[1,8]{1,0:T(1,128)} %param.24) | copy-start | bytes 100
Sparse Core Ops, SparseCore 0:
  130.7 34.3 all-reduce.3

commit v2 on v0

v2 whole, which is shorter than its diff:
```python
import functools
import math

import jax
import jax.numpy as jnp
from jax import lax
from jax.experimental import pallas as pl
from jax.experimental.pallas import tpu as pltpu
from jax.sharding import PartitionSpec as P

EPSILON = 1e-06
LANES = 128
GROUP = 32
FOLD = 8
PACK = 16
CHUNK = 1024
TINY = 1.1754944e-38
F32 = jnp.float32
BF16 = jnp.bfloat16
MESH = pl.DeviceIdType.MESH
LAST = (((1,), (1,)), ((), ()))
FIRST = (((0,), (0,)), ((), ()))


def lane_tiles(width):
    return [slice(t * LANES, (t + 1) * LANES) for t in range(width // LANES)]


def dot(a, b, dims=None, precision=None):
    if dims is None:
        dims = (((1,), (0,)), ((), ()))
    return lax.dot_general(a, b, dims, preferred_element_type=F32, precision=precision)


def kernel(
    seq_total,
    query_total,
    chan_total,
    lengths,
    slots,
    hidden,
    grad,
    step,
    proj,
    decay,
    skip,
    in_sketch,
    out_sketch,
    queries,
    scores,
    step_f,
    grad_f,
    states,
    local_y,
    mixed,
    out_table,
    in_table,
    in_diag,
    open_diag,
    reset,
    member,
    ends,
    inbox,
    outbox,
    in_own,
    in_peer,
    out_own,
    out_peer,
    sketch_part,
    sketch_peer,
    query_all,
    relay_send,
    relay_recv,
    pair_send,
    pair_recv,
    query_send,
    query_recv,
    sketch_send,
    sketch_recv,
):
    rows, channels = grad.shape
    count = decay.shape[0]
    docs = lengths.shape[1]
    owned = docs // seq_total
    side = LANES // owned
    chunks = channels // CHUNK
    tiles = lane_tiles(CHUNK)
    seq = lax.axis_index("seq")
    query = lax.axis_index("query")
    chan = lax.axis_index("chan")
    quarter = query * chan_total + chan
    team = query_total * chan_total

    def seq_peer(offset):
        return {"seq": lax.rem(seq + offset, seq_total)}

    def team_peer(offset):
        other = lax.rem(quarter + offset, team)
        return {"query": lax.div(other, chan_total), "chan": lax.rem(other, chan_total)}

    barrier = pltpu.get_barrier_semaphore()
    for offset in range(1, seq_total):
        pl.semaphore_signal(barrier, inc=1, device_id=seq_peer(offset), device_id_type=MESH)
    for offset in range(1, team):
        pl.semaphore_signal(barrier, inc=1, device_id=team_peer(offset), device_id_type=MESH)
    pl.semaphore_wait(barrier, seq_total + team - 2)

    def query_copy(offset):
        return pltpu.make_async_remote_copy(
            src_ref=queries,
            dst_ref=query_all.at[quarter],
            send_sem=query_send.at[offset - 1],
            recv_sem=query_recv.at[offset - 1],
            device_id=team_peer(offset),
            device_id_type=MESH,
        )

    def pair_copy(source, target, index):
        return pltpu.make_async_remote_copy(
            src_ref=source,
            dst_ref=target,
            send_sem=pair_send.at[index],
            recv_sem=pair_recv.at[index],
            device_id={"chan": 1 - chan},
            device_id_type=MESH,
        )

    def relay_copy(index):
        return pltpu.make_async_remote_copy(
            src_ref=outbox.at[index],
            dst_ref=inbox.at[index],
            send_sem=relay_send.at[index],
            recv_sem=relay_recv.at[index],
            device_id={"seq": lax.rem(seq + seq_total - 1, seq_total)},
            device_id_type=MESH,
        )

    def sketch_copy(offset):
        return pltpu.make_async_remote_copy(
            src_ref=sketch_part.at[lax.rem(seq + offset, seq_total)],
            dst_ref=sketch_peer.at[offset - 1],
            send_sem=sketch_send.at[offset - 1],
            recv_sem=sketch_recv.at[offset - 1],
            device_id=seq_peer(offset),
            device_id_type=MESH,
        )

    for offset in range(1, team):
        query_copy(offset).start()
    in_own[...] = dot(hidden[...], in_sketch[...], LAST)
    pair_copy(in_own, in_peer, 0).start()

    begin = seq * rows
    line = begin + lax.broadcasted_iota(jnp.int32, (rows, LANES), 0)
    lane_slot = lax.broadcasted_iota(jnp.int32, (rows, LANES), 1) // side

    def mark_starts(k, carry):
        start, is_start, is_shut, is_any = carry
        is_start = jnp.where(line == start, 1.0, is_start)
        inside = (start > line) & (start < begin + rows)
        is_shut = jnp.where(inside, 1.0, is_shut)
        first = jnp.full(is_any.shape, start, jnp.int32)
        held = (first >= begin) & (first < begin + rows)
        is_any = jnp.where(held, 1.0, is_any)
        return start + lengths[0, k], is_start, is_shut, is_any

    empty = jnp.zeros((rows, LANES), F32)
    _, is_start, is_shut, is_any = lax.fori_loop(
        0, docs, mark_starts, (jnp.int32(0), empty, empty, jnp.zeros((count, LANES), F32))
    )
    reset[...] = jnp.where(is_start > 0.0, jnp.inf, 0.0)
    keep_all = 1.0 - is_any
    is_open = 1.0 - is_shut

    def owner_mask(owner, _):
        def mark(k, carry):
            start, mask = carry
            stop = start + lengths[0, k]
            hit = (lane_slot + owner * owned == slots[0, k]) & (line >= start) & (line < stop)
            return stop, jnp.where(hit, 1.0, mask)

        _, mask = lax.fori_loop(0, docs, mark, (jnp.int32(0), empty))
        member[owner] = mask.astype(BF16)
        return 0

    lax.fori_loop(0, seq_total, owner_mask, 0)

    wide = (PACK * count, rows)
    row_place = lax.broadcasted_iota(jnp.int32, wide, 0) // count
    row_line = lax.broadcasted_iota(jnp.int32, wide, 1)
    ones = jnp.ones((rows, LANES), BF16)
    spreads = [jnp.concatenate([proj[i].astype(F32)] * PACK, axis=0) for i in range(2)]

    def fill_tables(group, _):
        here = pl.ds(pl.multiple_of(group * PACK * count, PACK * count), PACK * count)
        for table, spread in zip((in_table, out_table), spreads):
            picked = jnp.where(row_line == row_place + group * PACK, spread, 0.0).astype(BF16)
            table[here, :] = dot(picked, ones)
        return 0

    lax.fori_loop(0, rows // PACK, fill_tables, 0)

    deep = (rows, GROUP * FOLD)
    on_line = lax.rem(lax.broadcasted_iota(jnp.int32, deep, 0), GROUP) == (
        lax.broadcasted_iota(jnp.int32, deep, 1) // FOLD
    )
    diag = on_line.astype(F32)
    in_diag[...] = diag.astype(BF16)
    open_wide = jnp.concatenate([is_open] * (GROUP * FOLD // LANES), axis=1)
    open_diag[...] = (diag * open_wide).astype(BF16)

    def folded(value):
        parts = [value[i : i + FOLD] for i in range(0, count, FOLD)]
        return sum(parts[1:], parts[0])

    def rate_of(columns):
        return -jnp.maximum(decay[:, columns] * math.log2(math.e), TINY)

    def chunk_tiles(chunk):
        base = chunk * CHUNK
        return [pl.ds(pl.multiple_of(base + t * LANES, LANES), LANES) for t in range(len(tiles))]

    def relay(chunk):
        @pl.when(seq < seq_total - 1)
        def _():
            relay_copy(chunk).wait_recv()

        @pl.when(seq == seq_total - 1)
        def _():
            inbox[chunk] = jnp.zeros((count, CHUNK), F32)

        @pl.when(seq > 0)
        def _():
            here = pl.ds(pl.multiple_of(chunk * CHUNK, CHUNK), CHUNK)
            total = dot(jnp.ones((PACK, rows), BF16), step[:, here])
            keep = jnp.concatenate([keep_all] * len(tiles), axis=1)
            through = jnp.exp2(rate_of(here) * total[0:1, :]) * keep
            outbox[chunk] = through * inbox[chunk] + ends[chunk]
            relay_copy(chunk).start()

    after = seq_total - 1 - seq
    is_first = lax.div(after, seq_total - 1)
    is_far = lax.div(lax.div(after, chunks) + seq_total - 1, seq_total)
    late = is_first + is_far - is_first * is_far
    lag = late * chunks + (1 - late) * after

    def scan_chunk(chunk, _):
        here = pl.ds(pl.multiple_of(chunk * CHUNK, CHUNK), CHUNK)
        grad_f[...] = grad[:, here].astype(F32)
        for t, at in zip(tiles, chunk_tiles(chunk)):
            step_f[:, t] = step[:, at].astype(F32) + reset[...]
        rates = [rate_of(at) for at in chunk_tiles(chunk)]

        def one_group(index, carry):
            group = rows // GROUP - 1 - index
            first = pl.multiple_of(group * GROUP, GROUP)
            near_step = step_f.at[pl.ds(first, GROUP), :]
            near_grad = grad_f.at[pl.ds(first, GROUP), :]
            for pair in reversed(range(GROUP // 2)):
                sums = [None, None]
                for which in (1, 0):
                    offset = 2 * pair + which
                    at = pl.ds(pl.multiple_of((first + offset) * count, count), count)
                    weight, reader = out_table[at, :], in_table[at, :]
                    one = slice(offset, offset + 1)
                    fresh, sums[which] = [], []
                    for t, a, held in zip(tiles, rates, carry):
                        adjoint = weight * near_grad[one, t] + held
                        sums[which].append(folded(reader * adjoint))
                        fresh.append(jnp.exp2(near_step[one, t] * a) * adjoint)
                    carry = fresh
                for t, low, high in zip(tiles, *sums):
                    both = jnp.concatenate([low, high], axis=0)
                    states[pair * PACK : (pair + 1) * PACK, t] = both.astype(BF16)
            local_y[pl.ds(first, GROUP), here] = dot(in_diag[pl.ds(first, GROUP), :], states[...])
            return carry

        start = [jnp.zeros((count, LANES), F32) for _ in tiles]
        last = lax.fori_loop(0, rows // GROUP, one_group, start)
        for t, value in zip(tiles, last):
            ends[chunk, :, t] = value

        @pl.when(chunk >= lag)
        def _():
            relay(chunk - lag)

        return 0

    lax.fori_loop(0, chunks, scan_chunk, 0)
    out_own[...] = jnp.zeros_like(out_own)
    later = (
        lax.broadcasted_iota(jnp.int32, (rows, rows), 0)
        < lax.broadcasted_iota(jnp.int32, (rows, rows), 1)
    ).astype(F32).astype(BF16)

    def join_chunk(chunk, _):
        @pl.when(chunk < lag)
        def _():
            relay(chunks + chunk - lag)

        here = pl.ds(pl.multiple_of(chunk * CHUNK, CHUNK), CHUNK)
        step_f[...] = dot(later, step[:, here])
        rates = [rate_of(at) for at in chunk_tiles(chunk)]
        enters = [inbox[chunk, :, t] for t in tiles]

        def one_group(group, _):
            first = pl.multiple_of(group * GROUP, GROUP)
            near = step_f.at[pl.ds(first, GROUP), :]
            for pair in range(GROUP // 2):
                readers = []
                for offset in (2 * pair, 2 * pair + 1):
                    at = pl.ds(pl.multiple_of((first + offset) * count, count), count)
                    readers.append((slice(offset, offset + 1), in_table[at, :]))
                for t, a, e in zip(tiles, rates, enters):
                    both = jnp.concatenate(
                        [folded(jnp.exp2(near[one, t] * a) * e * b) for one, b in readers], axis=0
                    )
                    states[pair * PACK : (pair + 1) * PACK, t] = both.astype(BF16)
            lines = pl.ds(first, GROUP)
            total = local_y[lines, here] + dot(open_diag[lines, :], states[...])
            result = skip[:, here] * grad[lines, here].astype(F32) + step[lines, here].astype(
                F32
            ) * total
            mixed[lines, :] = result.astype(BF16)
            return 0

        lax.fori_loop(0, rows // GROUP, one_group, 0)
        out_own[...] += dot(out_sketch[:, here], mixed[...], LAST)
        return 0

    lax.fori_loop(0, chunks, join_chunk, 0)

    pair_copy(out_own, out_peer, 1).start()
    pair_copy(in_own, in_peer, 0).wait()
    in_side = (in_own[...] + in_peer[...]).astype(BF16)
    pair_copy(out_own, out_peer, 1).wait()
    out_side = (out_own[...] + out_peer[...]).astype(BF16)

    def one_owner(owner, _):
        sketch_part[owner] = dot(out_side, in_side * member[owner])
        return 0

    lax.fori_loop(0, seq_total, one_owner, 0)
    for offset in range(1, seq_total):
        sketch_copy(offset).start()

    @pl.when(seq > 0)
    def _():
        for chunk in range(chunks):
            relay_copy(chunk).wait_send()

    for offset in range(1, team):
        query_copy(offset).wait()
    query_all[quarter] = queries[...]
    total = sketch_part[seq]
    for offset in range(1, seq_total):
        sketch_copy(offset).wait()
        total += sketch_peer[offset - 1]

    entry = lax.broadcasted_iota(jnp.int32, (LANES, LANES), 0) // side
    same = (entry == lax.broadcasted_iota(jnp.int32, (LANES, LANES), 1) // side).astype(F32)
    squares = jnp.broadcast_to(jnp.sum(total * total, axis=0, keepdims=True), (8, LANES))
    mean_square = dot(squares, same, precision=lax.Precision.HIGHEST)[0:1] / (side * side)
    normed = (total * lax.rsqrt(mean_square + EPSILON)).astype(BF16).astype(F32)
    half = (
        lax.broadcasted_iota(jnp.int32, (8, LANES), 0)
        == lax.broadcasted_iota(jnp.int32, (8, LANES), 1) // side
    ).astype(F32)
    local_queries = queries.shape[0]
    for index in range(team):
        product = query_all[index].astype(F32) * normed[None]
        columns = jnp.sum(product, axis=1)
        value = dot(half, columns, LAST, precision=lax.Precision.HIGHEST)
        scores[:, index * local_queries : (index + 1) * local_queries] = value[:owned]


def local(
    hidden_rows,
    scan_grad,
    step_size,
    state_proj,
    decay_rate,
    skip_gain,
    in_sketch,
    out_sketch,
    doc_lengths,
    doc_slot,
    query_sketch,
):
    seq_total = lax.axis_size("seq")
    query_total = lax.axis_size("query")
    chan_total = lax.axis_size("chan")
    rows, channels = scan_grad.shape[1:]
    count = decay_rate.shape[0]
    docs = doc_lengths.shape[1]
    side = in_sketch.shape[1]
    owned = docs // seq_total
    chunks = channels // CHUNK
    team = query_total * chan_total
    local_queries = query_sketch.shape[0]
    square = query_sketch.reshape(local_queries, side, side)
    queries = jnp.concatenate([square] * owned, axis=2)
    in_wide = jnp.concatenate([in_sketch.T] * owned, axis=0)
    vmem = pl.BlockSpec(memory_space=pltpu.VMEM)
    smem = pl.BlockSpec(memory_space=pltpu.SMEM)
    dma = pltpu.SemaphoreType.DMA
    scores = pl.pallas_call(
        functools.partial(kernel, seq_total, query_total, chan_total),
        in_specs=[smem, smem] + [vmem] * 9,
        out_specs=vmem,
        out_shape=jax.ShapeDtypeStruct((owned, team * local_queries), F32),
        scratch_shapes=[
            pltpu.VMEM((rows, CHUNK), F32),
            pltpu.VMEM((rows, CHUNK), F32),
            pltpu.VMEM((GROUP * FOLD, CHUNK), BF16),
            pltpu.VMEM((rows, channels), F32),
            pltpu.VMEM((rows, CHUNK), BF16),
            pltpu.VMEM((rows * count, LANES), F32),
            pltpu.VMEM((rows * count, LANES), F32),
            pltpu.VMEM((rows, GROUP * FOLD), BF16),
            pltpu.VMEM((rows, GROUP * FOLD), BF16),
            pltpu.VMEM((rows, LANES), F32),
            pltpu.VMEM((seq_total, rows, LANES), BF16),
            pltpu.VMEM((chunks, count, CHUNK), F32),
            pltpu.VMEM((chunks, count, CHUNK), F32),
            pltpu.VMEM((chunks, count, CHUNK), F32),
            pltpu.VMEM((rows, LANES), F32),
            pltpu.VMEM((rows, LANES), F32),
            pltpu.VMEM((side, rows), F32),
            pltpu.VMEM((side, rows), F32),
            pltpu.VMEM((seq_total, side, LANES), F32),
            pltpu.VMEM((seq_total - 1, side, LANES), F32),
            pltpu.VMEM((team, local_queries, side, LANES), BF16),
            dma((chunks,)),
            dma((chunks,)),
            dma((2,)),
            dma((2,)),
            dma((team - 1,)),
            dma((team - 1,)),
            dma((seq_total - 1,)),
            dma((seq_total - 1,)),
        ],
        compiler_params=pltpu.CompilerParams(
            vmem_limit_bytes=52 * 2**20, collective_id=0, has_side_effects=True
        ),
        name="sketch_scores",
    )(
        doc_lengths,
        doc_slot,
        hidden_rows[0],
        scan_grad[0],
        step_size[0],
        state_proj[0],
        decay_rate,
        skip_gain[None, :],
        in_wide,
        out_sketch.T,
        queries,
    )
    return scores[None]


def solution(mesh):
    placed = (
        P(("groups", "query"), "seq", "chan"),
        P(("groups", "query"), "seq", "chan"),
        P(("groups", "query"), "seq", "chan"),
        P(("groups", "query"), None, None, "seq"),
        P(None, "chan"),
        P("chan"),
        P("chan", None),
        P("chan", None),
        P(("groups", "query"), None),
        P(("groups", "query"), None),
        P(("query", "chan"), None),
    )
    return jax.shard_map(
        local,
        mesh=mesh,
        in_specs=placed,
        out_specs=P(("groups", "query"), "seq", None),
        check_vma=False,
    )
```

time: 622 us -> 72.7 us (0.12); the launches traced: 609 us -> 72.3 us
  other arithmetic: 431 us -> 1.18 us
  local copies, waits for them, and re-layouts: 87.8 us -> 6.32 us
  Pallas kernels: 0 us -> 64.8 us
  waiting for transfers between devices: 53.8 us -> 0 us
  between operations: 13.6 us -> 0.04 us
  blocking collectives: 9.71 us -> 0 us
    reduce_sum x96 -> x0, other arithmetic: 196 us -> none  [the longest x64 182 us: one_turn(): jnp.sum(in_block[offset].astype(jnp.float32)[:, None] * adjoint, axis=0)]
    convert_element_type x161 -> x0, other arithmetic: 134 us -> none  [the longest x32 62.7 us: one_turn(): results[offset] = mixed.astype(jnp.bfloat16)]
    pallas_call x0 -> x1, Pallas kernels: none -> 64.8 us  [local(): pl.pallas_call(functools.partial(kernel, seq_total, query_total, chan_tot...]
    neg x33 -> x0, other arithmetic: 45.3 us -> none  [the longest x32 44.5 us: one_turn(): -step_f[None, :] * decay_rate]
    mul x34 -> x0, other arithmetic: 43.5 us -> none  [the longest x32 42.8 us: one_turn(): jnp.exp(-step_f[None, :] * decay_rate) * keep_block[offset] * adjoint]
    mul x65 -> x0, local copies, waits for them, and re-layouts: 29.8 us -> none  [the longest x32 29.4 us: add_block(): factor = jnp.exp(-decay_rate[None, :, :] * steps_block[:, None, :])]
    psum x1 -> x0, waiting for transfers between devices: 28.6 us -> none  [local(): summed = lax.psum(doc_partial, 'seq')]
    ppermute x3 -> x0, waiting for transfers between devices: 25.2 us -> none  [shifted(): return lax.ppermute(block, axis, route)]
  transfers between devices with their start and end apart: 4 -> 0, of which waited for: 4 -> 0; matrix products, arithmetic and copies ran while one was open for 0% -> 0% of each run, Pallas kernels for 0% -> 0%
where the time goes in v2:
time: 72.7 us; the launch traced here: 72.3 us
  Pallas kernels  64.8 us (89%)
  local copies, waits for them, and re-layouts  6.32 us (9%)
  other arithmetic  1.18 us (2%)
    pallas_call x1, Pallas kernels, local(): pl.pallas_call(functools.partial(kernel, seq_total, query_total, chan_tot...  64.8 us
    unnamed x13, local copies, waits for them, and re-layouts  5.29 us

profile of v2, /device:TPU:0, one launch (start us, length us, event | category | flops | bytes accessed | tf_op | source)
XLA Modules:
  0.0 72.3 jit_solution(10003251258352721999)
XLA Ops:
  0.0 1.0 %reshape.3 = bf16[8,64,64]{2,1,0:T(8,128)(2,1)S(1)} reshape(bf16[8,4096]{1,0:T(8,128)(2,1)} %param.21) | data formatting | bytes 131072 | tf_op jit(solution)/shard_map/reshape | solution.py:401
  1.0 0.1 pad_maximum_fusion.1.queries
  1.2 1.1 %pad_maximum_fusion.in_sketch = bf16[128,2048]{1,0:T(8,128)(2,1)S(1)} fusion(bf16[64,2048]{1,0:T(8,128)(2,1)} %bitcast.15), kind=kLoop, calls=%fused_computation | loop fusion | flops 1048576 | bytes 786432 | tf_op jit(solution)/shard_map/concatenate | solution.py:403
  2.2 0.0 copy-start
  2.2 1.0 %copy-done = bf16[4096,64]{0,1:T(8,128)(2,1)S(1)} copy-done((bf16[4096,64]{0,1:T(8,128)(2,1)S(1)}, bf16[4096,64]{0,1:T(8,128)(2,1)}, u32[]{:S(2)}) %copy-start) | copy-done | bytes 524312
  3.3 0.0 copy-start.1
  3.3 0.9 %copy-done.1 = f32[16,4096]{1,0:T(8,128)S(1)} copy-done((f32[16,4096]{1,0:T(8,128)S(1)}, f32[16,4096]{1,0:T(8,128)}, u32[]{:S(2)}) %copy-start.1) | copy-done | bytes 262168
  4.2 0.0 copy-start.2
  4.2 0.7 copy-done.2
  4.9 0.0 copy-start.3
  4.9 0.7 copy-done.3
  5.7 0.0 copy-start.4
  5.7 0.7 copy-done.4
  6.3 0.0 copy-start.5
  6.3 0.7 copy-done.5
  7.0 64.8 %sketch_scores.1 = f32[2,32]{1,0:T(2,128)S(1)} custom-call(s32[1,8]{1,0:T(1,128)S(1)} %copy-done.4, s32[1,8]{1,0:T(1,128)S(1)} %copy-done.5, bf16[256,2048]{1,0:T(8,128)(2,1)} %bitcast.14, bf16[256,4096]{1,0:T(8,128)(2,1)} %bitcast.12, bf16[256,4096]{1,0:T(8,128)(2,1)} %bitcast.13, bf16[2,16,256]{2,1,0:T(8,128)(2,1)S(1)} %bitcast.9, ...), custom_call_target="tpu_custom_call" | custom-call | tf_op jit(solution)/shard_map/sketch_scores/pallas_call | solution.py:407
  71.7 0.6 copy.13
Async XLA Ops:
  2.2 1.0 %copy-start = (bf16[4096,64]{0,1:T(8,128)(2,1)S(1)}, bf16[4096,64]{0,1:T(8,128)(2,1)}, u32[]{:S(2)}) copy-start(bf16[4096,64]{0,1:T(8,128)(2,1)} %param.18) | copy-start | bytes 1572868
  3.3 0.9 %copy-start.1 = (f32[16,4096]{1,0:T(8,128)S(1)}, f32[16,4096]{1,0:T(8,128)}, u32[]{:S(2)}) copy-start(f32[16,4096]{1,0:T(8,128)} %decay.1) | copy-start | bytes 786436
  4.2 0.7 copy-start.2
  4.9 0.7 copy-start.3
  5.7 0.7 copy-start.4
  6.3 0.7 copy-start.5

commit v3 on v2

--- a/solution.py
+++ b/solution.py
@@ -36,6 +36,18 @@
     seq_total,
     query_total,
     chan_total,
+    lengths_in,
+    slots_in,
+    hidden_in,
+    grad_in,
+    step_in,
+    proj_in,
+    decay_in,
+    skip_in,
+    in_sketch,
+    out_sketch_in,
+    queries,
+    scores,
     lengths,
     slots,
     hidden,
@@ -44,10 +56,7 @@
     proj,
     decay,
     skip,
-    in_sketch,
     out_sketch,
-    queries,
-    scores,
     step_f,
     grad_f,
     states,
@@ -77,6 +86,7 @@
     query_recv,
     sketch_send,
     sketch_recv,
+    load_sems,
 ):
     rows, channels = grad.shape
     count = decay.shape[0]
@@ -98,6 +108,25 @@
         other = lax.rem(quarter + offset, team)
         return {"query": lax.div(other, chan_total), "chan": lax.rem(other, chan_total)}
 
+    loads = [
+        pltpu.make_async_copy(source, target, load_sems.at[i])
+        for i, (source, target) in enumerate(
+            (
+                (lengths_in, lengths),
+                (slots_in, slots),
+                (proj_in, proj),
+                (hidden_in, hidden),
+                (decay_in, decay),
+                (step_in, step),
+                (grad_in, grad),
+                (skip_in, skip),
+                (out_sketch_in, out_sketch),
+            )
+        )
+    ]
+    for load in loads:
+        load.start()
+
     barrier = pltpu.get_barrier_semaphore()
     for offset in range(1, seq_total):
         pl.semaphore_signal(barrier, inc=1, device_id=seq_peer(offset), device_id_type=MESH)
@@ -147,9 +176,9 @@
 
     for offset in range(1, team):
         query_copy(offset).start()
-    in_own[...] = dot(hidden[...], in_sketch[...], LAST)
-    pair_copy(in_own, in_peer, 0).start()
-
+
+    for load in loads[:3]:
+        load.wait()
     begin = seq * rows
     line = begin + lax.broadcasted_iota(jnp.int32, (rows, LANES), 0)
     lane_slot = lax.broadcasted_iota(jnp.int32, (rows, LANES), 1) // side
@@ -212,6 +241,12 @@
     def folded(value):
         parts = [value[i : i + FOLD] for i in range(0, count, FOLD)]
         return sum(parts[1:], parts[0])
+
+    loads[3].wait()
+    in_own[...] = dot(hidden[...], in_sketch[...], LAST)
+    pair_copy(in_own, in_peer, 0).start()
+    for load in loads[4:]:
+        load.wait()
 
     def rate_of(columns):
         return -jnp.maximum(decay[:, columns] * math.log2(math.e), TINY)
@@ -402,14 +437,23 @@
     queries = jnp.concatenate([square] * owned, axis=2)
     in_wide = jnp.concatenate([in_sketch.T] * owned, axis=0)
     vmem = pl.BlockSpec(memory_space=pltpu.VMEM)
-    smem = pl.BlockSpec(memory_space=pltpu.SMEM)
+    anywhere = pl.BlockSpec(memory_space=pltpu.HBM)
     dma = pltpu.SemaphoreType.DMA
     scores = pl.pallas_call(
         functools.partial(kernel, seq_total, query_total, chan_total),
-        in_specs=[smem, smem] + [vmem] * 9,
+        in_specs=[anywhere] * 8 + [vmem, anywhere, vmem],
         out_specs=vmem,
         out_shape=jax.ShapeDtypeStruct((owned, team * local_queries), F32),
         scratch_shapes=[
+            pltpu.SMEM((1, docs), jnp.int32),
+            pltpu.SMEM((1, docs), jnp.int32),
+            pltpu.VMEM(hidden_rows.shape[1:], BF16),
+            pltpu.VMEM((rows, channels), BF16),
+            pltpu.VMEM((rows, channels), BF16),
+            pltpu.VMEM(state_proj.shape[1:], BF16),
+            pltpu.VMEM(decay_rate.shape, F32),
+            pltpu.VMEM((1, channels), F32),
+            pltpu.VMEM((side, channels), BF16),
             pltpu.VMEM((rows, CHUNK), F32),
             pltpu.VMEM((rows, CHUNK), F32),
             pltpu.VMEM((GROUP * FOLD, CHUNK), BF16),
@@ -439,9 +483,10 @@
             dma((team - 1,)),
             dma((seq_total - 1,)),
             dma((seq_total - 1,)),
+            dma((9,)),
         ],
         compiler_params=pltpu.CompilerParams(
-            vmem_limit_bytes=52 * 2**20, collective_id=0, has_side_effects=True
+            vmem_limit_bytes=64 * 2**20, collective_id=0, has_side_effects=True
         ),
         name="sketch_scores",
     )(

time: 72.7 us -> 69 us (0.949)
  local copies, waits for them, and re-layouts: 6.32 us -> 2.21 us
  other arithmetic: 1.18 us -> 2.63 us
  Pallas kernels: 64.8 us -> 63.9 us
    unnamed x13 -> x1, local copies, waits for them, and re-layouts: 5.29 us -> 1.18 us
    pallas_call x1, Pallas kernels: 64.8 us -> 63.9 us  [local(): pl.pallas_call(functools.partial(kernel, seq_total, query_total, chan_tot...]
    concatenate x1, other arithmetic: 1.07 us -> 1.86 us  [local(): in_wide = jnp.concatenate([in_sketch.T] * owned, axis=0)]
where the time goes in v3:
time: 69 us; the launch traced here: 68.8 us
  Pallas kernels  63.9 us (93%)
  other arithmetic  2.63 us (4%)
  local copies, waits for them, and re-layouts  2.21 us (3%)
    pallas_call x1, Pallas kernels, local(): pl.pallas_call(functools.partial(kernel, seq_total, query_total, chan_tot...  63.9 us
    concatenate x1, other arithmetic, local(): in_wide = jnp.concatenate([in_sketch.T] * owned, axis=0)  1.86 us

profile of v3, /device:TPU:0, one launch (start us, length us, event | category | flops | bytes accessed | tf_op | source)
XLA Modules:
  0.0 68.8 jit_solution(5560211574234417428)
XLA Ops:
  0.0 1.0 %reshape.3 = bf16[8,64,64]{2,1,0:T(8,128)(2,1)S(1)} reshape(bf16[8,4096]{1,0:T(8,128)(2,1)} %param.21) | data formatting | bytes 131072 | tf_op jit(solution)/shard_map/reshape | solution.py:436
  1.0 0.8 %pad_maximum_fusion.1.queries = bf16[8,64,128]{2,1,0:T(8,128)(2,1)} fusion(bf16[8,64,64]{2,1,0:T(8,128)(2,1)S(1)} %reshape.3), kind=kLoop, calls=%fused_computation.1 | loop fusion | flops 262144 | bytes 196608 | tf_op jit(solution)/shard_map/concatenate | solution.py:437
  1.8 1.9 %pad_maximum_fusion.in_sketch = bf16[128,2048]{1,0:T(8,128)(2,1)} fusion(bf16[64,2048]{1,0:T(8,128)(2,1)} %bitcast.12), kind=kLoop, calls=%fused_computation | loop fusion | flops 1048576 | bytes 786432 | tf_op jit(solution)/shard_map/concatenate | solution.py:438
  3.7 63.9 %sketch_scores.1 = f32[2,32]{1,0:T(2,128)} custom-call(s32[1,8]{1,0:T(1,128)} %lengths_in.1, s32[1,8]{1,0:T(1,128)} %slots_in.1, bf16[256,2048]{1,0:T(8,128)(2,1)} %bitcast.10, bf16[256,4096]{1,0:T(8,128)(2,1)} %bitcast.8, bf16[256,4096]{1,0:T(8,128)(2,1)} %bitcast.9, bf16[2,16,256]{2,1,0:T(8,128)(2,1)} %bitcast.13, f32[16,4096]{1,0:T(8,128)} %decay_in.1, ...), custom_call_target="tpu_custom_call" | custom-call | tf_op jit(solution)/shard_map/sketch_scores/pallas_call | solution.py:442
  67.6 1.2 %copy.13 = f32[1,2,32]{2,1,0:T(2,128)} copy(f32[1,2,32]{2,1,0:T(2,128)} %bitcast.15) | data formatting | bytes 512
